TPU v7x, 32 devices: a whole 2x2x4 slice. The times are simulated.
32 devices in a mesh: row: 4 (over z), col: 8 (over y, x, core).
Axes of the slice: x: 2, y: 2, z: 4, core: 2. Of those that a mesh axis runs over, the one named last changes fastest.
Arguments:
- densities: bfloat16 [7680, 4500], P('col'), may hold values from -0.75 to 0.75
- coupling_a: float32 [5, 900], replicated, may hold values from -6 to 6
- coupling_b: float32 [5, 900], replicated, may hold values from -6 to 6
- energies: float32 [7680], replicated, may hold values from 2 to 40
- strength: float32 [7680], replicated, may hold values from -6 to 6
- qp_index: int32 [7680, 2], replicated, may hold values from 0 to 1023
- kpi_label: int32 [7680], replicated, may hold values from 0 to 15
- amplitude_u: float32 [1024], replicated, may hold values from 0.1 to 1
- amplitude_v: float32 [1024], replicated, may hold values from 0.1 to 1
- panel_blocks: int32 [2], replicated, may hold values from 0 to 3, as said below
Outputs:
- matrix_a: float32 [2, 960, 7680], P(None, 'row', 'col')
- matrix_b: float32 [2, 960, 7680], P(None, 'row', 'col')
- response: float32 [2, 960], P(None, 'row')
- mirror: float32 [2, 7680], P(None, 'col')
Inputs may be any that keep to these rules, and one draw needn't show every extreme that they name: `panel_blocks`: both blocks lie in the lower half of the column blocks, one of them is block 3, and the two may coincide.
All inputs are finite; a program needn't handle non-finite values.
Results may differ from a plain program's by a relative error of at most 0.007.
Values may be sent and summed in bfloat16 or wider, within the bound.
No kernel may reach another device: no remote copies, remote signals or barrier semaphores. Data moves between devices by JAX's collectives and lax.ppermute only.
A program may use at most 64 MiB of HBM per device.

v0:
```python
import functools
import math

import jax
import jax.numpy as jnp
from jax import lax
from jax.experimental import pallas as pl
from jax.experimental.pallas import tpu as pltpu
from jax.sharding import PartitionSpec as P

PAIRING = 1.0
HIGH = lax.Precision.HIGHEST
LANES = 128
PIECES = 2
PIECES_ONCE = 4
FIELDS = 8
FACT_TILE = 256
BRANCHES = 4
IN_VMEM = pl.BlockSpec(memory_space=pltpu.VMEM)
IN_SMEM = pl.BlockSpec(memory_space=pltpu.SMEM)
ANYWHERE = pl.BlockSpec(memory_space=pl.ANY)

OWN, R1, R2, R3, R4 = 1, 2, 3, 4, 5
SRC_O, SRC_TOP, _, ACT_O, ACT_TOP, PANEL_O, PANEL_TOP, START_O, START_TOP, COL_POS, ROW_POS = (
    0, 2, 4, 5, 6, 7, 8, 9, 10, 11, 12,
)
BUSY, SEED = 13, 14
FIRST, SECOND, LABEL, STRENGTH, ENERGY = 0, 1, 2, 3, 4
ANOMAL, DIRECT = 0, 1


def up(size, step):
    return -(-size // step) * step


def vmem(value):
    return pltpu.with_memory_space_constraint(value, pltpu.VMEM)


def times(left, right):
    return lax.dot_general(
        left, right, (((1,), (1,)), ((), ())), preferred_element_type=jnp.float32
    )


def with_factors(facts, table):
    size = facts.shape[1]
    highs = table.shape[0] // 2
    low_ids = lax.broadcasted_iota(jnp.int32, (LANES, size), 0)
    high_ids = lax.broadcasted_iota(jnp.int32, (highs, size), 0)
    amps = []
    for field in (FIRST, SECOND):
        state = facts[field : field + 1].astype(jnp.int32)
        low = (low_ids == state % LANES).astype(jnp.float32)
        high = (high_ids == state // LANES).astype(jnp.float32)
        both = jnp.dot(table, low, precision=HIGH, preferred_element_type=jnp.float32)
        amps.append(jnp.sum(both[:highs] * high, axis=0, keepdims=True))
        amps.append(jnp.sum(both[highs:] * high, axis=0, keepdims=True))
    anomal = amps[0] * amps[3] + amps[1] * amps[2]
    direct = amps[0] * amps[2] - amps[1] * amps[3]
    return jnp.concatenate([anomal, direct, facts[2:]], axis=0)


def stretch(packed, start, size):
    window = up(size, LANES) + LANES
    base = pl.multiple_of(start // LANES * LANES, LANES)
    return pltpu.roll(packed[:, pl.ds(base, window)], window - start % LANES, 1)[:, :size]


def facts_kernel(spans, flags, packed, table, dens, cols, rows, *rest):
    gathered = rest[-1] if not spans else rest[-3]
    if spans:
        cut_pieces(spans, flags, dens, rest[:-3], *rest[-2:])
    block_len, row_len = cols.shape[1], rows.shape[1]
    places = [(flags[COL_POS] * block_len, block_len)]
    for slot in range(2):
        start = flags[START_O + slot] * block_len + flags[ROW_POS] * row_len
        places.append((start, row_len))
    at = 0
    gathered[...] = jnp.zeros_like(gathered)
    spots = []
    for start, size in places:
        gathered[:, at : at + size] = stretch(packed, start, size)
        spots.append(at)
        at += up(size, FACT_TILE)

    def step(i, carry):
        span = pl.ds(pl.multiple_of(i * FACT_TILE, FACT_TILE), FACT_TILE)
        gathered[:, span] = with_factors(gathered[:, span], table[...])
        return carry

    lax.fori_loop(0, gathered.shape[1] // FACT_TILE, step, 0)
    cols[...] = gathered[:, :block_len]
    for slot in range(2):
        facts = gathered[:, spots[1 + slot] : spots[1 + slot] + row_len]
        rows[slot] = jnp.concatenate([facts] * (LANES // FIELDS), axis=0).T


def cut_pieces(spans, flags, dens, pieces, buf, sem):
    rows = buf.shape[0]
    lo, hi = spans[0][0], spans[-1][1]
    source = dens.at[pl.ds(flags[ROW_POS] * rows, rows), pl.ds(lo, hi - lo)]
    copy = pltpu.make_async_copy(source, buf, sem)
    copy.start()
    copy.wait()
    for (start, end), piece in zip(spans, pieces):
        width = piece.shape[1]

        def step(i, carry):
            span = pl.ds(pl.multiple_of(i * 16, 16), 16)
            if end - start < width:
                piece[span, :] = jnp.zeros((16, width), piece.dtype)
            piece[span, : end - start] = buf[span, start - lo : end - lo]
            return carry

        lax.fori_loop(0, rows // 16, step, 0)


def cut_kernel(spans, flags, dens, *rest):
    cut_pieces(spans, flags, dens, rest[:-2], *rest[-2:])


def by_bands(source, target):
    rows = source.shape[0]
    band = 16 if rows % 16 == 0 else rows

    def step(i, carry):
        span = pl.ds(pl.multiple_of(i * band, 16), band) if band < rows else slice(0, rows)
        target[span, :] = source[span, :]
        return carry

    lax.fori_loop(0, rows // band, step, 0)


def pass_kernel(value, token, same):
    by_bands(value, same)


def seed_kernel(flags, value, instead, token, same):
    @pl.when(flags[SEED] > 0)
    def _():
        by_bands(instead, same)

    @pl.when(flags[SEED] == 0)
    def _():
        by_bands(value, same)


def row_tile(rows):
    return 48 if rows % 48 == 0 else rows


def weigh(x, at_lane, weights, start, width, lhs, base):
    rows = x.shape[0]
    tile = row_tile(rows)
    step_rows = up(rows, 16)

    def step(i, carry):
        at = 0 if tile == rows else pl.multiple_of(i * tile, 16)
        values = x[pl.ds(at, tile), pl.ds(at_lane, width)].astype(jnp.float32)
        for which in range(2):
            scale = weights[which : which + 1, pl.ds(start, width)]
            spot = pl.ds(base + which * step_rows + at, tile)
            lhs[spot, :width] = (values * scale).astype(jnp.bfloat16)
        return carry

    if tile == rows:
        step(0, 0)
    else:
        lax.fori_loop(0, rows // tile, step, 0)


def gather(entry, sources, flags, weights, span, lhs, base):
    for code, ref in sources:

        @pl.when(flags[entry] == code)
        def _():
            weigh(ref, 0, weights, span[0], span[1] - span[0], lhs, base)


def work(steps, flags, dens, weights, before, acc, lhs, arrival=None):
    block = acc.shape[0] // 2
    width = lhs.shape[2]
    together = all(pieces[0][1] == pieces[1][1] for pieces in steps)
    rows = 2 * block if together else block
    parts = []
    for c, pieces in enumerate(steps):
        for n, (entry, span, sources) in enumerate(pieces):
            if together:
                gather(entry, sources, flags, weights, span, lhs.at[c], n * block)
            else:
                gather(entry, sources, flags, weights, span, lhs.at[2 * c + n], 0)
                parts.append(span)
        if together:
            parts.append(pieces[0][1])
    if before is None:
        sub = width // 2 if width % (2 * LANES) == 0 else width
        acc[...] = jnp.zeros_like(acc)
        arrival.wait()

        def step(i, carry):
            start = pl.multiple_of(parts[0][0] + i * sub, LANES)
            at = pl.multiple_of(i % (width // sub) * sub, LANES)
            acc[:rows] += times(
                lhs[i // (width // sub), :rows, pl.ds(at, sub)], dens[:, pl.ds(start, sub)]
            )
            return carry

        lax.fori_loop(0, len(parts) * (width // sub), step, 0)
        return
    total = before[:rows]
    for i, (lo, hi) in enumerate(parts):
        total = total + times(lhs[i, :rows, : hi - lo], dens[:, lo:hi])
    acc[:rows] = total


def spelled(plan, refs):
    return [
        [(entry, span, [(c, refs[r]) for c, r in found]) for entry, span, found in pieces]
        for pieces in plan
    ]


def first_kernel(plan, cut, count, flags, *rest):
    dens_from, weights, _, acc, token, dens, lhs, sems = rest[count:]
    ends = (pl.ds(0, cut), pl.ds(cut, dens.shape[1] - cut))
    copies = [
        pltpu.make_async_copy(dens_from.at[:, span], dens.at[:, span], sems.at[n])
        for n, span in enumerate(ends)
    ]

    @pl.when(flags[BUSY] > 0)
    def _():
        for copy in copies:
            copy.start()
        work(spelled(plan, rest[:count]), flags, dens, weights, None, acc, lhs, copies[0])
        copies[1].wait()

    token[...] = jnp.zeros_like(token)


def last_kernel(plan, twice, count, flags, *rest):
    refs = rest[:count]
    dens, weights, cols, rows, before = rest[count : count + 5]
    mat_a, mat_b, resp, mirror, acc, sums, lhs, made, out_sems = rest[count + 5 :]

    @pl.when(flags[BUSY] > 0)
    def _():
        work(spelled(plan, refs), flags, dens, weights, before, acc, lhs)

    block = acc.shape[0] // 2
    row_len, block_len = made.shape[2:]
    row_pad = block // 2
    tile = 48 if row_len % 48 == 0 else row_len
    resp[...] = jnp.zeros_like(resp)
    mirror[...] = jnp.zeros_like(mirror)

    def out_copies(slot, panel, at):
        return [
            pltpu.make_async_copy(made.at[slot, 0], mat_a.at[panel], out_sems.at[at, 0]),
            pltpu.make_async_copy(made.at[slot, 1], mat_b.at[panel], out_sems.at[at, 1]),
        ]

    def finish(slot, carry):
        panel = flags[PANEL_O + slot]

        @pl.when(flags[ACT_O + slot] > 0)
        def _():
            row_start = flags[START_O + slot] * block_len + flags[ROW_POS] * row_len
            shift = row_start - flags[COL_POS] * block_len

            def band(i, total):
                at = i * tile if tile == row_len else pl.multiple_of(i * tile, 16)
                span = pl.ds(at, tile)
                row = rows[slot, span, :]
                row_ids = lax.broadcasted_iota(jnp.int32, (tile, block_len), 0)
                col_ids = lax.broadcasted_iota(jnp.int32, (tile, block_len), 1)
                same = row[:, LABEL : LABEL + 1] == cols[LABEL : LABEL + 1]
                pair_a = row[:, ANOMAL : ANOMAL + 1] * cols[ANOMAL : ANOMAL + 1]
                pair_b = row[:, DIRECT : DIRECT + 1] * cols[DIRECT : DIRECT + 1]
                on_diagonal = row_ids + (at + shift) == col_ids
                full_a = acc[pl.ds(slot * block + at, tile), :] + jnp.where(same, PAIRING * pair_a, 0.0)
                full_a = full_a + jnp.where(on_diagonal, row[:, ENERGY : ENERGY + 1], 0.0)
                full_b = acc[pl.ds(slot * block + row_pad + at, tile), :]
                full_b = full_b + jnp.where(same, PAIRING * pair_b, 0.0)
                made[slot, 0, span, :] = full_a
                made[slot, 1, span, :] = full_b
                both = full_a + full_b
                across = jnp.sum(both * cols[STRENGTH : STRENGTH + 1], axis=1, keepdims=True)
                sums[span, :] = jnp.broadcast_to(across, (tile, LANES))
                return total + jnp.sum(both * row[:, STRENGTH : STRENGTH + 1], axis=0, keepdims=True)

            total = jnp.zeros((1, block_len), jnp.float32)
            if tile == row_len:
                total = band(0, total)
            else:
                total = lax.fori_loop(0, row_len // tile, band, total)
            mirror[pl.ds(panel, 1), :] = total
            resp[pl.ds(panel, 1), :] = sums[...].T[0:1]

        @pl.when(flags[ACT_O + slot] == 0)
        def _():
            made[slot] = jnp.zeros(made.shape[1:], made.dtype)

        for copy in out_copies(slot, panel, slot):
            copy.start()
        return carry

    if twice:
        finish(0, 0)
        for copy in out_copies(0, flags[PANEL_TOP], 1):
            copy.start()
        resp[pl.ds(flags[PANEL_TOP], 1), :] = resp[pl.ds(flags[PANEL_O], 1), :]
        mirror[pl.ds(flags[PANEL_TOP], 1), :] = mirror[pl.ds(flags[PANEL_O], 1), :]
    else:
        lax.fori_loop(0, 2, finish, 0)
    for slot in range(2):
        for copy in out_copies(0 if twice else slot, flags[PANEL_O + slot], slot):
            copy.wait()


def limit(mebibytes):
    return pltpu.CompilerParams(vmem_limit_bytes=mebibytes << 20)


def cost(flops, moved):
    return pl.CostEstimate(flops=flops, bytes_accessed=moved, transcendentals=0)


def all_sum(value, axis):
    size = lax.axis_size(axis)
    if size & (size - 1):
        return lax.psum(value, axis)
    step = 1
    while step < size:
        value = value + lax.ppermute(value, axis, [(i, i ^ step) for i in range(size)])
        step *= 2
    return value


def on_device(
    densities,
    coupling_a,
    coupling_b,
    energies,
    strength,
    qp_index,
    kpi_label,
    amplitude_u,
    amplitude_v,
    panel_blocks,
):
    block_len, depth = densities.shape
    row_count = lax.axis_size("row")
    cols = lax.axis_size("col")
    half = cols // 2
    top = half - 1
    row_len = block_len // row_count
    row_pad = up(row_len, 16)
    row_pos = lax.axis_index("row")
    col_pos = lax.axis_index("col")
    total_pairs = block_len * cols
    row_start = row_pos * row_len
    other = panel_blocks[0] + panel_blocks[1] - top
    top_panel = jnp.where(panel_blocks[0] == top, 0, 1)

    upper = col_pos >= half
    even_chip = (col_pos // 2) % 2 == 0

    def code(on_even, parity):
        direct = even_chip if on_even else ~even_chip
        holds = col_pos % 2 == parity
        return jnp.where(holds, jnp.where(direct, R1, R2), jnp.where(direct, R3, R4))

    def code_o(parity):
        same_quad = jnp.where(col_pos % 2 == parity, R2, R4)
        near = jnp.where(col_pos // 2 == other // 2, R3, same_quad)
        if cols > 8:
            near = jnp.int32(R1)
        low = jnp.where(col_pos == other, OWN, jnp.where(col_pos < other, 0, near))
        return jnp.where(upper, code(True, parity), low)

    def code_top(parity):
        return jnp.where(upper, code(False, parity), jnp.where(col_pos == top, OWN, 0))

    flags = jnp.stack(
        [
            code_o(0),
            code_o(1),
            code_top(0),
            code_top(1),
            jnp.int32(0),
            col_pos >= other,
            col_pos >= top,
            1 - top_panel,
            top_panel,
            other,
            jnp.int32(top),
            col_pos,
            row_pos,
            col_pos >= other,
            jnp.where(other == top, upper & ~even_chip, col_pos == other),
        ]
    ).astype(jnp.int32)

    in_kernels = row_len % 16 == 0

    def spans_of(count):
        width = up(-(-depth // count), LANES)
        return [(lo, min(depth, lo + width)) for lo in range(0, depth, width)]

    def cut(spans):
        width = spans[0][1]
        if in_kernels:
            ahead = spans[: len(spans) // 2]
            return pl.pallas_call(
                functools.partial(cut_kernel, ahead),
                out_shape=[pltpu.VMEM((row_len, width), densities.dtype) for _ in ahead],
                in_specs=[IN_SMEM, ANYWHERE],
                out_specs=[IN_VMEM for _ in ahead],
                scratch_shapes=cut_scratch(ahead),
                compiler_params=limit(6),
                name="cut",
            )(flags, densities)
        return sliced(spans)

    def sliced(spans):
        width = spans[0][1]
        parts = [lax.dynamic_slice(densities, (row_start, lo), (row_len, hi - lo)) for lo, hi in spans]
        return [jnp.pad(x, ((0, 0), (0, width - x.shape[1]))) for x in parts]

    def cut_scratch(spans):
        return [
            pltpu.VMEM((row_len, spans[-1][1] - spans[0][0]), densities.dtype),
            pltpu.SemaphoreType.DMA,
        ]

    def seeded(o, came, own, token):
        value, instead = (came[0], own) if o != top else came
        if cols > 8:
            return jnp.where(flags[SEED] > 0, instead, value)
        return pl.pallas_call(
            seed_kernel,
            out_shape=pltpu.VMEM(value.shape, value.dtype),
            in_specs=[IN_SMEM] + [IN_VMEM] * 3,
            out_specs=IN_VMEM,
            input_output_aliases={1: 0},
            compiler_params=limit(4),
            cost_estimate=cost(1, 1),
            name="seed",
        )(flags, vmem(value), vmem(instead), token)

    def to_chips(o, value, q):
        pairs = [(half + q, half + 2 + q), (half + 2 + q, half + q)]
        if o % 4 < 2 and o < top:
            pairs.append((o, o // 4 * 4 + 2 + q))
        return lax.ppermute(value, "col", pairs)

    def to_cores(o, value, q, with_o):
        pairs = [(half + q, half + 1 - q), (half + 2 + q, half + 3 - q)]
        if with_o and o % 2 == 0 and o < top:
            pairs.append((o, o + 1))
        if not with_o and o % 4 < 2 and o < top:
            pairs.append((o // 4 * 4 + 2 + q, o // 4 * 4 + 3 - q))
        return lax.ppermute(value, "col", pairs)

    def everywhere(o, value, r2, r3, r4, q):
        holds = col_pos % 2 == q
        now = [jnp.where(holds, value, r3), jnp.where(holds, r2, r4)]
        for quad in range(1, cols // 8):
            here = half + 4 * quad
            pairs = [(here - 4 + j, here + j) for j in range(4)]
            inside = (col_pos >= here) & (col_pos < here + 4)
            now = [jnp.where(inside, lax.ppermute(x, "col", pairs), x) for x in now]
        low = jnp.where(col_pos // 2 == o // 2, r3, now[1])
        later = range(o // 4 * 4 + 4, half, 4)
        for at in later:
            low = jnp.where(col_pos == at, lax.ppermute(value, "col", [(o, at)]), low)
        if later:
            beyond = col_pos >= later[0]
            got = lax.ppermute(low, "col", [(at, at + 1) for at in later])
            low = jnp.where(beyond & (col_pos % 4 == 1), got, low)
            pairs = [(at + j, at + j + 2) for at in later for j in range(2)]
            low = jnp.where(beyond & (col_pos % 4 >= 2), lax.ppermute(low, "col", pairs), low)
        first = jnp.where(upper, now[0], low)
        return [first, now[1], first, now[1]]

    def out_of_block(o, pieces, once):
        if o != top:
            return [
                [lax.ppermute(x, "col", [(o, half + i % 2), (top, half + 2 + i % 2)])]
                for i, x in enumerate(pieces)
            ]
        pairs = list(zip(pieces[0::2], pieces[1::2])) if once else [(x, x) for x in pieces]
        got = []
        for i, (one, two) in enumerate(pairs):
            to_even = lax.ppermute(one, "col", [(top, half + i % 2)])
            to_odd = lax.ppermute(two, "col", [(top, half + 2 + i % 2)])
            got.append([to_even, to_odd])
        return got

    def after(value, token):
        return pl.pallas_call(
            pass_kernel,
            out_shape=pltpu.VMEM(value.shape, value.dtype),
            in_specs=[IN_VMEM] * 2,
            out_specs=IN_VMEM,
            input_output_aliases={0: 0},
            compiler_params=limit(4),
            cost_estimate=cost(1, 1),
            name="after",
        )(vmem(value), token)

    def facts(spans, width):
        pairs = [qp_index[:, 0], qp_index[:, 1], kpi_label, strength, energies]
        pairs += [jnp.zeros_like(strength)] * (FIELDS - len(pairs))
        packed = jnp.stack([x.astype(jnp.float32) for x in pairs])
        packed = jnp.pad(packed, ((0, 0), (0, 2 * LANES)))
        table = jnp.concatenate([amplitude_u.reshape(-1, LANES), amplitude_v.reshape(-1, LANES)])
        gathered = pltpu.VMEM(
            (FIELDS, up(block_len, FACT_TILE) + 2 * up(row_len, FACT_TILE)), jnp.float32
        )
        return pl.pallas_call(
            functools.partial(facts_kernel, spans),
            out_shape=[
                pltpu.VMEM((FIELDS, block_len), jnp.float32),
                pltpu.VMEM((2, row_len, LANES), jnp.float32),
            ]
            + [pltpu.VMEM((row_len, width), densities.dtype) for _ in spans],
            in_specs=[IN_SMEM] + [IN_VMEM] * 2 + [ANYWHERE],
            out_specs=[IN_VMEM] * (2 + len(spans)),
            scratch_shapes=[gathered] + (cut_scratch(spans) if spans else []),
            compiler_params=limit(8),
            cost_estimate=cost(1, 1),
            name="facts",
        )(flags, packed, table, densities)

    def computed(o, spans, pieces, came, col_facts, row_facts, twice):
        weights = vmem(jnp.stack([coupling_a.reshape(-1), coupling_b.reshape(-1)]))
        acc_shape = pltpu.VMEM((4 * row_pad, block_len), jnp.float32)
        lhs_rows = 2 * row_pad if twice else 4 * row_pad
        lhs_shape = pltpu.VMEM((2 if twice else 1, lhs_rows, spans[0][1]), jnp.bfloat16)
        count = len(came)
        got = [list(arrays) for arrays in came]

        def plan_of(chunks):
            refs, plan = [], []
            for i in chunks:
                base = len(refs)
                refs += got[i]
                found = [(R1, base), (R2, base + 1), (R3, base + 2), (R4, base + 3)]
                own = [2 * i, 2 * i + 1] if twice else [i, i]
                step = []
                for which, p in zip((SRC_O, SRC_TOP), own):
                    step.append((which + i % 2, spans[p], [(OWN, len(refs))] + found))
                    refs.append(pieces[p])
                plan.append(step)
            return refs, plan

        refs, plan = plan_of(range(count - 1))
        ins = [flags, *[vmem(x) for x in refs], densities, weights, col_facts]
        ahead = spans[len(spans) - len(spans) // count][0]
        acc, token, dens = pl.pallas_call(
            functools.partial(first_kernel, plan, ahead, len(refs)),
            out_shape=[
                acc_shape,
                pltpu.VMEM((8, LANES), jnp.float32),
                pltpu.VMEM(densities.shape, densities.dtype),
            ],
            in_specs=[IN_SMEM] + [IN_VMEM] * len(refs) + [ANYWHERE] + [IN_VMEM] * 2,
            out_specs=[IN_VMEM] * 3,
            scratch_shapes=[lhs_shape, pltpu.SemaphoreType.DMA((2,))],
            compiler_params=limit(16),
            cost_estimate=cost(1, 1),
            name="first",
        )(*ins)
        if len(got[-1]) < 4:
            got[-1][1] = after(got[-1][1], token)
            got[-1].append(to_cores(o, got[-1][1], (count - 1) % 2, False))
        refs, plan = plan_of([count - 1])
        mat = jax.ShapeDtypeStruct((2, row_len, block_len), jnp.float32)
        ins = [flags, *[vmem(x) for x in refs], dens, weights, col_facts, row_facts, acc]
        mat_a, mat_b, resp, mirror, _ = pl.pallas_call(
            functools.partial(last_kernel, plan, twice, len(refs)),
            out_shape=[
                mat,
                mat,
                jax.ShapeDtypeStruct((2, row_len), jnp.float32),
                jax.ShapeDtypeStruct((2, block_len), jnp.float32),
                acc_shape,
            ],
            in_specs=[IN_SMEM] + [IN_VMEM] * (len(ins) - 1),
            out_specs=[ANYWHERE, ANYWHERE] + [IN_VMEM] * 3,
            scratch_shapes=[
                pltpu.VMEM((row_len, LANES), jnp.float32),
                lhs_shape,
                pltpu.VMEM((2, 2, row_len, block_len), jnp.float32),
                pltpu.SemaphoreType.DMA((2, 2)),
            ],
            input_output_aliases={len(ins) - 1: 4},
            compiler_params=limit(18),
            cost_estimate=cost(8 * row_len * block_len * spans[0][1], 16 * row_len * block_len),
            name="last",
        )(*ins)
        return mat_a, mat_b, resp, mirror

    def summed(mat_a, mat_b, resp, mirror):
        response = all_sum(resp, "col") * (1.0 / math.sqrt(total_pairs))
        mirror = all_sum(mirror, "row") * (1.0 / math.sqrt(block_len))
        return mat_a, mat_b, response, mirror

    def spread(o, i, value):
        q = i % 2
        return value, to_chips(o, value, q), to_cores(o, value, q, True)

    def branch(o):
        spans = spans_of(PIECES_ONCE if o == top else PIECES)
        width = spans[0][1]
        pieces = list(cut(spans))
        col_facts, row_facts, *others = facts(spans[len(pieces) :], width)
        pieces += others
        came = out_of_block(o, pieces, True)
        spreads = [
            list(spread(o, i, seeded(o, x, pieces[i], col_facts))) for i, x in enumerate(came)
        ]
        for i, now in enumerate(spreads[:-1]):
            now.append(to_cores(o, now[1], i % 2, False))
        return computed(o, spans, pieces, spreads, col_facts, row_facts, o == top)

    if half <= BRANCHES:
        return summed(*lax.switch(other, [functools.partial(branch, o) for o in range(half)]))
    spans = spans_of(PIECES)
    pieces = cut(spans) if not in_kernels else sliced(spans)

    def transfers(o):
        spreads = []
        for i, x in enumerate(out_of_block(o, pieces, False)):
            value = seeded(o, x, pieces[i], None)
            value, r2, r3 = spread(o, i, value)
            r4 = to_cores(o, r2, i % 2, False)
            spreads.append(everywhere(o, value, r2, r3, r4, i % 2))
        return spreads

    came = lax.switch(other, [functools.partial(transfers, o) for o in range(half)])
    col_facts, row_facts = facts([], 0)
    return summed(*computed(None, spans, pieces, came, col_facts, row_facts, False))


def solution(mesh):
    placed = (P("col", None), P(), P(), P(), P(), P(), P(), P(), P(), P())
    return jax.shard_map(
        on_device,
        mesh=mesh,
        in_specs=placed,
        out_specs=(P(None, "row", "col"), P(None, "row", "col"), P(None, "row"), P(None, "col")),
        check_vma=False,
    )
```

profile of v0, /device:TPU:0, one launch (start us, length us, event | category | flops | bytes accessed | tf_op | source)
XLA Modules:
  0.0 67.6 jit_solution(8377879039491383370)
XLA Ops:
  0.7 1.3 %fusion = (s32[1]{0:T(128)}, s32[1]{0:T(128)}) fusion(s32[2]{0:T(128)} %param.23), kind=kLoop, calls=%fused_computation.18 | loop fusion | bytes 16 | tf_op jit(solution)/shard_map/slice | solution.py:364
  4.1 0.1 stack.123
  4.2 23.6 %conditional.1 = (f32[2,240,960]{2,1,0:T(8,128)}, f32[2,240,960]{2,1,0:T(8,128)}, f32[2,240]{1,0:T(2,128)S(1)}, f32[2,960]{1,0:T(2,128)S(1)}) conditional(s32[]{:T(128)} %clamp.3, (s32[7680,2]{0,1:T(2,128)}, s32[7680]{0:T(1024)}, f32[7680]{0:T(1024)}, f32[7680]{0:T(1024)}, f32[1024]{0:T(1024)}, ...), branch_computations={%region_0.1_spmd, %region_1.2_spmd, %region_2.3_spmd, %region_3.4_... | conditional | flops 4246766848 | bytes 43446152 | solution.py:631
  4.5 2.0 %cut.7 = (bf16[240,1152]{1,0:T(8,128)(2,1)S(1)}, bf16[240,1152]{1,0:T(8,128)(2,1)S(1)}) custom-call(s32[15]{0:T(128)S(1)} %get-tuple-element.140.flags, bf16[960,4500]{1,0:T(8,128)(2,1)} %get-tuple-element.147.dens.rest_6_), custom_call_target="tpu_custom_call" | custom-call | tf_op jit(solution)/shard_map/cond/branch_3_fun/cut/pallas_call | solution.py:416
  6.5 0.7 %collective-permute-start.27 = (bf16[240,1152]{1,0:T(8,128)(2,1)S(1)}, bf16[240,1152]{1,0:T(8,128)(2,1)S(1)}, u32[]{:S(2)}, u32[]{:S(2)}) collective-permute-start(bf16[240,1152]{1,0:T(8,128)(2,1)S(1)} %get-tuple-element.151.rest_4_), channel_id=1, source_target_pairs={{3,4},{11,12},{19,20},{27,28}} | collective-permute-start | bytes 1658888 | tf_op jit(solution)/shard_map/cond/branch_3_fun/ppermute | solution.py:497
  7.2 1.5 %collective-permute-start.28 = (bf16[240,1152]{1,0:T(8,128)(2,1)S(1)}, bf16[240,1152]{1,0:T(8,128)(2,1)}, u32[]{:S(2)}, u32[]{:S(2)}) collective-permute-start(bf16[240,1152]{1,0:T(8,128)(2,1)S(1)} %get-tuple-element.152.rest_5_), channel_id=1, source_target_pairs={{3,6},{11,14},{19,22},{27,30}} | collective-permute-start | bytes 1658888 | tf_op jit(solution)/shard_map/cond/branch_3_fun/ppermute | solution.py:498
  8.9 0.3 stack.96
  9.3 3.9 %facts.7 = (f32[8,960]{1,0:T(8,128)S(1)}, f32[2,240,128]{2,1,0:T(8,128)S(1)}, bf16[240,1152]{1,0:T(8,128)(2,1)S(1)}, bf16[240,1152]{1,0:T(8,128)(2,1)S(1)}) custom-call(s32[15]{0:T(128)S(1)} %get-tuple-element.140.flags, f32[8,7936]{1,0:T(8,128)S(1)} %pad.12.packed, f32[16,128]{1,0:T(8,128)S(1)} %pad_maximum_fusion.7.table, ...), custom_call_target="tpu_custom_call" | custom-call | flops 1 | bytes 1 | tf_op jit(solution)/shard_map/cond/branch_3_fun/facts/pallas_call | solution.py:523
  13.2 0.8 %collective-permute-start.24 = (bf16[240,1152]{1,0:T(8,128)(2,1)S(1)}, bf16[240,1152]{1,0:T(8,128)(2,1)S(1)}, u32[]{:S(2)}, u32[]{:S(2)}) collective-permute-start(bf16[240,1152]{1,0:T(8,128)(2,1)S(1)} %get-tuple-element.148.rest_4_), channel_id=1, source_target_pairs={{3,5},{11,13},{19,21},{27,29}} | collective-permute-start | bytes 1658888 | tf_op jit(solution)/shard_map/cond/branch_3_fun/ppermute | solution.py:497
  14.1 1.5 %collective-permute-start.25 = (bf16[240,1152]{1,0:T(8,128)(2,1)S(1)}, bf16[240,1152]{1,0:T(8,128)(2,1)}, u32[]{:S(2)}, u32[]{:S(2)}) collective-permute-start(bf16[240,1152]{1,0:T(8,128)(2,1)S(1)} %get-tuple-element.149.rest_5_), channel_id=1, source_target_pairs={{3,7},{11,15},{19,23},{27,31}} | collective-permute-start | bytes 1658888 | tf_op jit(solution)/shard_map/cond/branch_3_fun/ppermute | solution.py:498
  15.5 1.2 %seed.15.rest_0_ = bf16[240,1152]{1,0:T(8,128)(2,1)S(1)} custom-call(s32[15]{0:T(128)S(1)} %get-tuple-element.140.flags, bf16[240,1152]{1,0:T(8,128)(2,1)S(1)} %collective-permute-done.27.value, bf16[240,1152]{1,0:T(8,128)(2,1)} %collective-permute-done.28.instead, f32[8,960]{1,0:T(8,128)S(1)} %get-tuple-element.150.token.rest_8_), custom_call_target="tpu_custom_call", output_to_operand_aliasing={{}: (1, {})} | custom-call | flops 1 | bytes 1 | tf_op jit(solution)/shard_map/cond/branch_3_fun/seed/pallas_call | solution.py:442
  16.7 1.5 %collective-permute-start.29 = (bf16[240,1152]{1,0:T(8,128)(2,1)S(1)}, bf16[240,1152]{1,0:T(8,128)(2,1)}, u32[]{:S(2)}, u32[]{:S(2)}) collective-permute-start(bf16[240,1152]{1,0:T(8,128)(2,1)S(1)} %seed.15.rest_0_), channel_id=1, source_target_pairs={{4,6},{6,4},{12,14},{14,12},{20,22},{22,20},{28,30},{30,28}} | collective-permute-start | bytes 1658888 | tf_op jit(solution)/shard_map/cond/branch_3_fun/ppermute | solution.py:457
  18.2 0.1 reshape.155
  18.3 0.1 reshape.156
  18.4 0.7 %collective-permute-start.30 = (bf16[240,1152]{1,0:T(8,128)(2,1)S(1)}, bf16[240,1152]{1,0:T(8,128)(2,1)S(1)}, u32[]{:S(2)}, u32[]{:S(2)}) collective-permute-start(bf16[240,1152]{1,0:T(8,128)(2,1)S(1)} %seed.15.rest_0_), channel_id=1, source_target_pairs={{4,5},{6,7},{12,13},{14,15},{20,21},{22,23},{28,29},{30,31}} | collective-permute-start | bytes 1658888 | tf_op jit(solution)/shard_map/cond/branch_3_fun/ppermute | solution.py:465
  19.2 1.2 %seed.14.rest_0_ = bf16[240,1152]{1,0:T(8,128)(2,1)S(1)} custom-call(s32[15]{0:T(128)S(1)} %get-tuple-element.140.flags, bf16[240,1152]{1,0:T(8,128)(2,1)S(1)} %collective-permute-done.24.value, bf16[240,1152]{1,0:T(8,128)(2,1)} %collective-permute-done.25.instead, f32[8,960]{1,0:T(8,128)S(1)} %get-tuple-element.150.token.rest_8_), custom_call_target="tpu_custom_call", output_to_operand_aliasing={{}: (1, {})} | custom-call | flops 1 | bytes 1 | tf_op jit(solution)/shard_map/cond/branch_3_fun/seed/pallas_call | solution.py:442
  20.4 0.7 %collective-permute-start.26 = (bf16[240,1152]{1,0:T(8,128)(2,1)S(1)}, bf16[240,1152]{1,0:T(8,128)(2,1)S(1)}, u32[]{:S(2)}, u32[]{:S(2)}) collective-permute-start(bf16[240,1152]{1,0:T(8,128)(2,1)S(1)} %seed.14.rest_0_), channel_id=1, source_target_pairs={{5,7},{7,5},{13,15},{15,13},{21,23},{23,21},{29,31},{31,29}} | collective-permute-start | bytes 1658888 | tf_op jit(solution)/shard_map/cond/branch_3_fun/ppermute | solution.py:457
  21.1 0.7 %collective-permute-start.31 = (bf16[240,1152]{1,0:T(8,128)(2,1)}, bf16[240,1152]{1,0:T(8,128)(2,1)S(1)}, u32[]{:S(2)}, u32[]{:S(2)}) collective-permute-start(bf16[240,1152]{1,0:T(8,128)(2,1)} %collective-permute-done.29.rest_1_), channel_id=1, source_target_pairs={{4,5},{6,7},{12,13},{14,15},{20,21},{22,23},{28,29},{30,31}} | collective-permute-start | bytes 1658888 | tf_op jit(solution)/shard_map/cond/branch_3_fun/ppermute | solution.py:465
  21.8 0.7 %collective-permute-start.32 = (bf16[240,1152]{1,0:T(8,128)(2,1)S(1)}, bf16[240,1152]{1,0:T(8,128)(2,1)S(1)}, u32[]{:S(2)}, u32[]{:S(2)}) collective-permute-start(bf16[240,1152]{1,0:T(8,128)(2,1)S(1)} %seed.14.rest_0_), channel_id=1, source_target_pairs={{5,4},{7,6},{13,12},{15,14},{21,20},{23,22},{29,28},{31,30}} | collective-permute-start | bytes 1658888 | tf_op jit(solution)/shard_map/cond/branch_3_fun/ppermute | solution.py:465
  22.6 1.4 %first.7 = (f32[960,960]{1,0:T(8,128)S(1)}, f32[8,128]{1,0:T(8,128)S(1)}, bf16[960,4500]{1,0:T(8,128)(2,1)S(1)}) custom-call(s32[15]{0:T(128)S(1)} %get-tuple-element.140.flags, bf16[240,1152]{1,0:T(8,128)(2,1)S(1)} %seed.15.rest_0_, bf16[240,1152]{1,0:T(8,128)(2,1)} %collective-permute-done.29.rest_1_, ...), custom_call_target="tpu_custom_call" | custom-call | flops 1 | bytes 1 | tf_op jit(solution)/shard_map/cond/branch_3_fun/first/pallas_call | solution.py:563
  23.9 0.1 after.7.rest_1_
  24.1 0.7 %collective-permute-start.33 = (bf16[240,1152]{1,0:T(8,128)(2,1)S(1)}, bf16[240,1152]{1,0:T(8,128)(2,1)S(1)}, u32[]{:S(2)}, u32[]{:S(2)}) collective-permute-start(bf16[240,1152]{1,0:T(8,128)(2,1)S(1)} %after.7.rest_1_), channel_id=1, source_target_pairs={{5,4},{7,6},{13,12},{15,14},{21,20},{23,22},{29,28},{31,30}} | collective-permute-start | bytes 1658888 | tf_op jit(solution)/shard_map/cond/branch_3_fun/ppermute | solution.py:465
  24.9 2.6 %last.7 = (f32[2,240,960]{2,1,0:T(8,128)}, f32[2,240,960]{2,1,0:T(8,128)}, f32[2,240]{1,0:T(2,128)S(1)}, f32[2,960]{1,0:T(2,128)S(1)}, f32[960,960]{1,0:T(8,128)S(1)}) custom-call(s32[15]{0:T(128)S(1)} %get-tuple-element.140.flags, bf16[240,1152]{1,0:T(8,128)(2,1)S(1)} %seed.14.rest_0_, ...), custom_call_target="tpu_custom_call", output_to_operand_aliasing={{4}: (11, {})} | custom-call | flops 2123366400 | bytes 3686400 | tf_op jit(solution)/shard_map/cond/branch_3_fun/last/pallas_call | solution.py:583
  27.8 3.1 %collective-permute-start.37 = (f32[2,960]{1,0:T(2,128)S(1)}, f32[2,960]{1,0:T(2,128)S(1)}, u32[]{:S(2)}, u32[]{:S(2)}) collective-permute-start(f32[2,960]{1,0:T(2,128)S(1)} %get-tuple-element.174), channel_id=1, source_target_pairs={{0,8},{8,0},{16,24},{24,16},{1,9},{9,1},{17,25},{25,17},{2,10},{10... | collective-permute-start | bytes 23048 | tf_op jit(solution)/shard_map/ppermute | solution.py:336
  30.9 1.2 %collective-permute-done.34 = f32[2,240]{1,0:T(2,128)S(1)} collective-permute-done((f32[2,240]{1,0:T(2,128)S(1)}, f32[2,240]{1,0:T(2,128)S(1)}, u32[]{:S(2)}, u32[]{:S(2)}) %collective-permute-start.34) | collective-permute-done | bytes 1952 | tf_op jit(solution)/shard_map/ppermute | solution.py:336
  32.1 17.3 %collective-permute-start.35 = (f32[2,240]{1,0:T(2,128)S(1)}, f32[2,240]{1,0:T(2,128)S(1)}, u32[]{:S(2)}, u32[]{:S(2)}) collective-permute-start(f32[2,240]{1,0:T(2,128)S(1)} %add.46), channel_id=1, source_target_pairs={{0,2},{1,3},{2,0},{3,1},{4,6},{5,7},{6,4},{7,5},{8,10},{9,11},{10,... | collective-permute-start | bytes 5768 | tf_op jit(solution)/shard_map/ppermute | solution.py:336
  49.4 1.6 %collective-permute-done.35 = f32[2,240]{1,0:T(2,128)S(1)} collective-permute-done((f32[2,240]{1,0:T(2,128)S(1)}, f32[2,240]{1,0:T(2,128)S(1)}, u32[]{:S(2)}, u32[]{:S(2)}) %collective-permute-start.35) | collective-permute-done | bytes 1952 | tf_op jit(solution)/shard_map/ppermute | solution.py:336
  50.9 11.4 %collective-permute-start.36 = (f32[2,240]{1,0:T(2,128)S(1)}, f32[2,240]{1,0:T(2,128)S(1)}, u32[]{:S(2)}, u32[]{:S(2)}) collective-permute-start(f32[2,240]{1,0:T(2,128)S(1)} %add.47), channel_id=1, source_target_pairs={{0,4},{1,5},{2,6},{3,7},{4,0},{5,1},{6,2},{7,3},{8,12},{9,13},{10,... | collective-permute-start | bytes 5768 | tf_op jit(solution)/shard_map/ppermute | solution.py:336
  62.3 2.7 %collective-permute-start.38 = (f32[2,960]{1,0:T(2,128)S(1)}, f32[2,960]{1,0:T(2,128)S(1)}, u32[]{:S(2)}, u32[]{:S(2)}) collective-permute-start(f32[2,960]{1,0:T(2,128)S(1)} %add.49), channel_id=1, source_target_pairs={{0,16},{8,24},{16,0},{24,8},{1,17},{9,25},{17,1},{25,9},{2,18},{10... | collective-permute-start | bytes 23048 | tf_op jit(solution)/shard_map/ppermute | solution.py:336
  65.0 0.6 add_multiply_fusion.1
  65.6 1.4 %collective-permute-done.38 = f32[2,960]{1,0:T(2,128)S(1)} collective-permute-done((f32[2,960]{1,0:T(2,128)S(1)}, f32[2,960]{1,0:T(2,128)S(1)}, u32[]{:S(2)}, u32[]{:S(2)}) %collective-permute-start.38) | collective-permute-done | bytes 7712 | tf_op jit(solution)/shard_map/ppermute | solution.py:336
  66.9 0.6 add_multiply_fusion
  (46 shorter events, 0.4 us)
Async XLA Ops:
  4.4 4.2 %copy-start.11 = (s32[7680,2]{0,1:T(2,128)S(1)}, s32[7680,2]{0,1:T(2,128)}, u32[]{:S(2)}) copy-start(s32[7680,2]{0,1:T(2,128)} %get-tuple-element.141) | copy-start | bytes 184324 | tf_op jit(solution)/shard_map/cond
  4.4 4.3 %copy-start.19 = (f32[7680]{0:T(1024)S(1)}, f32[7680]{0:T(1024)}, u32[]{:S(2)}) copy-start(f32[7680]{0:T(1024)} %get-tuple-element.143) | copy-start | bytes 92164 | tf_op jit(solution)/shard_map/cond
  4.4 4.3 %copy-start.23 = (f32[7680]{0:T(1024)S(1)}, f32[7680]{0:T(1024)}, u32[]{:S(2)}) copy-start(f32[7680]{0:T(1024)} %get-tuple-element.144) | copy-start | bytes 92164 | tf_op jit(solution)/shard_map/cond
  4.5 4.3 %copy-start.15 = (s32[7680]{0:T(1024)S(1)}, s32[7680]{0:T(1024)}, u32[]{:S(2)}) copy-start(s32[7680]{0:T(1024)} %get-tuple-element.142) | copy-start | bytes 92164 | tf_op jit(solution)/shard_map/cond
  4.5 4.8 %copy-start.35 = (f32[1024]{0:T(1024)S(1)}, f32[1024]{0:T(1024)}, u32[]{:S(2)}) copy-start(f32[1024]{0:T(1024)} %get-tuple-element.145) | copy-start | bytes 12292 | tf_op jit(solution)/shard_map/cond
  4.5 4.8 %copy-start.39 = (f32[1024]{0:T(1024)S(1)}, f32[1024]{0:T(1024)}, u32[]{:S(2)}) copy-start(f32[1024]{0:T(1024)} %get-tuple-element.146) | copy-start | bytes 12292 | tf_op jit(solution)/shard_map/cond
  6.5 9.1 %collective-permute-start.27 = (bf16[240,1152]{1,0:T(8,128)(2,1)S(1)}, bf16[240,1152]{1,0:T(8,128)(2,1)S(1)}, u32[]{:S(2)}, u32[]{:S(2)}) collective-permute-start(bf16[240,1152]{1,0:T(8,128)(2,1)S(1)} %get-tuple-element.151.rest_4_), channel_id=1, source_target_pairs={{3,4},{11,12},{19,20},{27,28}} | collective-permute-start | bytes 1658888 | tf_op jit(solution)/shard_map/cond/branch_3_fun/ppermute | solution.py:497
  7.2 8.4 %collective-permute-start.28 = (bf16[240,1152]{1,0:T(8,128)(2,1)S(1)}, bf16[240,1152]{1,0:T(8,128)(2,1)}, u32[]{:S(2)}, u32[]{:S(2)}) collective-permute-start(bf16[240,1152]{1,0:T(8,128)(2,1)S(1)} %get-tuple-element.152.rest_5_), channel_id=1, source_target_pairs={{3,6},{11,14},{19,22},{27,30}} | collective-permute-start | bytes 1658888 | tf_op jit(solution)/shard_map/cond/branch_3_fun/ppermute | solution.py:498
  13.2 3.5 %copy-start.6 = (f32[2,240,128]{2,1,0:T(8,128)}, f32[2,240,128]{2,1,0:T(8,128)S(1)}, u32[]{:S(2)}) copy-start(f32[2,240,128]{2,1,0:T(8,128)S(1)} %get-tuple-element.157.rest_9_) | copy-start | bytes 737284 | tf_op jit(solution)/shard_map/cond
  13.2 5.0 %copy-start.27 = (f32[5,900]{1,0:T(8,128)S(1)}, f32[5,900]{1,0:T(8,128)}, u32[]{:S(2)}) copy-start(f32[5,900]{1,0:T(8,128)} %get-tuple-element.153) | copy-start | bytes 54004 | tf_op jit(solution)/shard_map/cond
  13.2 5.1 %copy-start.31 = (f32[5,900]{1,0:T(8,128)S(1)}, f32[5,900]{1,0:T(8,128)}, u32[]{:S(2)}) copy-start(f32[5,900]{1,0:T(8,128)} %get-tuple-element.154) | copy-start | bytes 54004 | tf_op jit(solution)/shard_map/cond
  13.2 5.9 %collective-permute-start.24 = (bf16[240,1152]{1,0:T(8,128)(2,1)S(1)}, bf16[240,1152]{1,0:T(8,128)(2,1)S(1)}, u32[]{:S(2)}, u32[]{:S(2)}) collective-permute-start(bf16[240,1152]{1,0:T(8,128)(2,1)S(1)} %get-tuple-element.148.rest_4_), channel_id=1, source_target_pairs={{3,5},{11,13},{19,21},{27,29}} | collective-permute-start | bytes 1658888 | tf_op jit(solution)/shard_map/cond/branch_3_fun/ppermute | solution.py:497
  14.1 5.1 %collective-permute-start.25 = (bf16[240,1152]{1,0:T(8,128)(2,1)S(1)}, bf16[240,1152]{1,0:T(8,128)(2,1)}, u32[]{:S(2)}, u32[]{:S(2)}) collective-permute-start(bf16[240,1152]{1,0:T(8,128)(2,1)S(1)} %get-tuple-element.149.rest_5_), channel_id=1, source_target_pairs={{3,7},{11,15},{19,23},{27,31}} | collective-permute-start | bytes 1658888 | tf_op jit(solution)/shard_map/cond/branch_3_fun/ppermute | solution.py:498
  16.7 4.3 %collective-permute-start.29 = (bf16[240,1152]{1,0:T(8,128)(2,1)S(1)}, bf16[240,1152]{1,0:T(8,128)(2,1)}, u32[]{:S(2)}, u32[]{:S(2)}) collective-permute-start(bf16[240,1152]{1,0:T(8,128)(2,1)S(1)} %seed.15.rest_0_), channel_id=1, source_target_pairs={{4,6},{6,4},{12,14},{14,12},{20,22},{22,20},{28,30},{30,28}} | collective-permute-start | bytes 1658888 | tf_op jit(solution)/shard_map/cond/branch_3_fun/ppermute | solution.py:457
  18.4 4.1 %collective-permute-start.30 = (bf16[240,1152]{1,0:T(8,128)(2,1)S(1)}, bf16[240,1152]{1,0:T(8,128)(2,1)S(1)}, u32[]{:S(2)}, u32[]{:S(2)}) collective-permute-start(bf16[240,1152]{1,0:T(8,128)(2,1)S(1)} %seed.15.rest_0_), channel_id=1, source_target_pairs={{4,5},{6,7},{12,13},{14,15},{20,21},{22,23},{28,29},{30,31}} | collective-permute-start | bytes 1658888 | tf_op jit(solution)/shard_map/cond/branch_3_fun/ppermute | solution.py:465
  20.4 3.6 %collective-permute-start.26 = (bf16[240,1152]{1,0:T(8,128)(2,1)S(1)}, bf16[240,1152]{1,0:T(8,128)(2,1)S(1)}, u32[]{:S(2)}, u32[]{:S(2)}) collective-permute-start(bf16[240,1152]{1,0:T(8,128)(2,1)S(1)} %seed.14.rest_0_), channel_id=1, source_target_pairs={{5,7},{7,5},{13,15},{15,13},{21,23},{23,21},{29,31},{31,29}} | collective-permute-start | bytes 1658888 | tf_op jit(solution)/shard_map/cond/branch_3_fun/ppermute | solution.py:457
  21.1 1.5 %collective-permute-start.31 = (bf16[240,1152]{1,0:T(8,128)(2,1)}, bf16[240,1152]{1,0:T(8,128)(2,1)S(1)}, u32[]{:S(2)}, u32[]{:S(2)}) collective-permute-start(bf16[240,1152]{1,0:T(8,128)(2,1)} %collective-permute-done.29.rest_1_), channel_id=1, source_target_pairs={{4,5},{6,7},{12,13},{14,15},{20,21},{22,23},{28,29},{30,31}} | collective-permute-start | bytes 1658888 | tf_op jit(solution)/shard_map/cond/branch_3_fun/ppermute | solution.py:465
  21.8 2.9 %collective-permute-start.32 = (bf16[240,1152]{1,0:T(8,128)(2,1)S(1)}, bf16[240,1152]{1,0:T(8,128)(2,1)S(1)}, u32[]{:S(2)}, u32[]{:S(2)}) collective-permute-start(bf16[240,1152]{1,0:T(8,128)(2,1)S(1)} %seed.14.rest_0_), channel_id=1, source_target_pairs={{5,4},{7,6},{13,12},{15,14},{21,20},{23,22},{29,28},{31,30}} | collective-permute-start | bytes 1658888 | tf_op jit(solution)/shard_map/cond/branch_3_fun/ppermute | solution.py:465
  23.9 0.9 %copy-start.7 = (f32[2,240,128]{2,1,0:T(8,128)S(1)}, f32[2,240,128]{2,1,0:T(8,128)}, u32[]{:S(2)}) copy-start(f32[2,240,128]{2,1,0:T(8,128)} %copy-done.6) | copy-start | bytes 737284 | tf_op jit(solution)/shard_map/cond
  24.1 0.7 %collective-permute-start.33 = (bf16[240,1152]{1,0:T(8,128)(2,1)S(1)}, bf16[240,1152]{1,0:T(8,128)(2,1)S(1)}, u32[]{:S(2)}, u32[]{:S(2)}) collective-permute-start(bf16[240,1152]{1,0:T(8,128)(2,1)S(1)} %after.7.rest_1_), channel_id=1, source_target_pairs={{5,4},{7,6},{13,12},{15,14},{21,20},{23,22},{29,28},{31,30}} | collective-permute-start | bytes 1658888 | tf_op jit(solution)/shard_map/cond/branch_3_fun/ppermute | solution.py:465
  27.8 34.5 %collective-permute-start.37 = (f32[2,960]{1,0:T(2,128)S(1)}, f32[2,960]{1,0:T(2,128)S(1)}, u32[]{:S(2)}, u32[]{:S(2)}) collective-permute-start(f32[2,960]{1,0:T(2,128)S(1)} %get-tuple-element.174), channel_id=1, source_target_pairs={{0,8},{8,0},{16,24},{24,16},{1,9},{9,1},{17,25},{25,17},{2,10},{10... | collective-permute-start | bytes 23048 | tf_op jit(solution)/shard_map/ppermute | solution.py:336
  30.9 1.2 %collective-permute-start.34 = (f32[2,240]{1,0:T(2,128)S(1)}, f32[2,240]{1,0:T(2,128)S(1)}, u32[]{:S(2)}, u32[]{:S(2)}) collective-permute-start(f32[2,240]{1,0:T(2,128)S(1)} %get-tuple-element.173), channel_id=1, source_target_pairs={{0,1},{1,0},{2,3},{3,2},{4,5},{5,4},{6,7},{7,6},{8,9},{9,8},{10,11... | collective-permute-start | bytes 5768 | tf_op jit(solution)/shard_map/ppermute | solution.py:336
  32.1 18.9 %collective-permute-start.35 = (f32[2,240]{1,0:T(2,128)S(1)}, f32[2,240]{1,0:T(2,128)S(1)}, u32[]{:S(2)}, u32[]{:S(2)}) collective-permute-start(f32[2,240]{1,0:T(2,128)S(1)} %add.46), channel_id=1, source_target_pairs={{0,2},{1,3},{2,0},{3,1},{4,6},{5,7},{6,4},{7,5},{8,10},{9,11},{10,... | collective-permute-start | bytes 5768 | tf_op jit(solution)/shard_map/ppermute | solution.py:336
  50.9 14.1 %collective-permute-start.36 = (f32[2,240]{1,0:T(2,128)S(1)}, f32[2,240]{1,0:T(2,128)S(1)}, u32[]{:S(2)}, u32[]{:S(2)}) collective-permute-start(f32[2,240]{1,0:T(2,128)S(1)} %add.47), channel_id=1, source_target_pairs={{0,4},{1,5},{2,6},{3,7},{4,0},{5,1},{6,2},{7,3},{8,12},{9,13},{10,... | collective-permute-start | bytes 5768 | tf_op jit(solution)/shard_map/ppermute | solution.py:336
  62.3 4.6 %collective-permute-start.38 = (f32[2,960]{1,0:T(2,128)S(1)}, f32[2,960]{1,0:T(2,128)S(1)}, u32[]{:S(2)}, u32[]{:S(2)}) collective-permute-start(f32[2,960]{1,0:T(2,128)S(1)} %add.49), channel_id=1, source_target_pairs={{0,16},{8,24},{16,0},{24,8},{1,17},{9,25},{17,1},{25,9},{2,18},{10... | collective-permute-start | bytes 23048 | tf_op jit(solution)/shard_map/ppermute | solution.py:336
where the time goes:
time: 68.1 us; the launch traced here: 67.6 us
  starting transfers between devices  43.9 us (64%)
  Pallas kernels  12.4 us (18%)
  waiting for transfers between devices  4.12 us (6%)
  between operations  2.78 us (4%)
  local copies, waits for them, and re-layouts  2.18 us (3%)
  other arithmetic  1.29 us (2%)
  loops' own time  0.95 us (1%)
    ppermute x5, starting transfers between devices, all_sum(): lax.ppermute(value, axis, [(i, i ^ step) for i in range(size)])  34.4 us
    ppermute x5, waiting for transfers between devices, all_sum(): lax.ppermute(value, axis, [(i, i ^ step) for i in range(size)])  4.09 us
    pallas_call x1, Pallas kernels, facts(): pl.pallas_call(functools.partial(facts_kernel, spans), out_shape=[pltpu.V...  3.9 us
    ppermute x2, starting transfers between devices, out_of_block(): to_odd = lax.ppermute(two, 'col', [(top, half + 2 + i % 2)])  2.95 us
    ppermute x4, starting transfers between devices, to_cores(): return lax.ppermute(value, 'col', pairs)  2.79 us
    pallas_call x1, Pallas kernels, computed(): pl.pallas_call(functools.partial(last_kernel, plan, twice, len(refs)), ou...  2.65 us
    pallas_call x2, Pallas kernels, seeded(): pl.pallas_call(seed_kernel, out_shape=pltpu.VMEM(value.shape, value.dtype...  2.37 us
    ppermute x2, starting transfers between devices, to_chips(): return lax.ppermute(value, 'col', pairs)  2.18 us
  transfers between devices with their start and end apart: 15, of which 3 were waited for; matrix products, arithmetic and copies ran while one was open for 2% of the time, Pallas kernels for 11%

commit v1 on v0

--- a/solution.py
+++ b/solution.py
@@ -327,15 +327,23 @@
     return pl.CostEstimate(flops=flops, bytes_accessed=moved, transcendentals=0)
 
 
-def all_sum(value, axis):
-    size = lax.axis_size(axis)
-    if size & (size - 1):
-        return lax.psum(value, axis)
+def both_sums(one, one_axis, two, two_axis):
+    sizes = [lax.axis_size(one_axis), lax.axis_size(two_axis)]
+    if any(size & (size - 1) for size in sizes):
+        return lax.psum(one, one_axis), lax.psum(two, two_axis)
+    length = one.shape[1]
+    room = up(length, LANES)
+    now = jnp.concatenate([jnp.pad(one, ((0, 0), (0, room - length))), two], axis=1)
     step = 1
-    while step < size:
-        value = value + lax.ppermute(value, axis, [(i, i ^ step) for i in range(size)])
+    while step < max(sizes):
+        parts = []
+        for part, axis, size in ((now[:, :room], one_axis, sizes[0]), (now[:, room:], two_axis, sizes[1])):
+            if step < size:
+                part = part + lax.ppermute(part, axis, [(i, i ^ step) for i in range(size)])
+            parts.append(part)
+        now = jnp.concatenate(parts, axis=1)
         step *= 2
-    return value
+    return now[:, :length], now[:, room:]
 
 
 def on_device(
@@ -456,13 +464,8 @@
             pairs.append((o, o // 4 * 4 + 2 + q))
         return lax.ppermute(value, "col", pairs)
 
-    def to_cores(o, value, q, with_o):
-        pairs = [(half + q, half + 1 - q), (half + 2 + q, half + 3 - q)]
-        if with_o and o % 2 == 0 and o < top:
-            pairs.append((o, o + 1))
-        if not with_o and o % 4 < 2 and o < top:
-            pairs.append((o // 4 * 4 + 2 + q, o // 4 * 4 + 3 - q))
-        return lax.ppermute(value, "col", pairs)
+    def to_cores(value):
+        return lax.ppermute(value, "col", [(i, i ^ 1) for i in range(cols)])
 
     def everywhere(o, value, r2, r3, r4, q):
         holds = col_pos % 2 == q
@@ -576,7 +579,7 @@
         )(*ins)
         if len(got[-1]) < 4:
             got[-1][1] = after(got[-1][1], token)
-            got[-1].append(to_cores(o, got[-1][1], (count - 1) % 2, False))
+            got[-1].append(to_cores(got[-1][1]))
         refs, plan = plan_of([count - 1])
         mat = jax.ShapeDtypeStruct((2, row_len, block_len), jnp.float32)
         ins = [flags, *[vmem(x) for x in refs], dens, weights, col_facts, row_facts, acc]
@@ -605,13 +608,13 @@
         return mat_a, mat_b, resp, mirror
 
     def summed(mat_a, mat_b, resp, mirror):
-        response = all_sum(resp, "col") * (1.0 / math.sqrt(total_pairs))
-        mirror = all_sum(mirror, "row") * (1.0 / math.sqrt(block_len))
-        return mat_a, mat_b, response, mirror
+        response, mirror = both_sums(resp, "col", mirror, "row")
+        response = response * (1.0 / math.sqrt(total_pairs))
+        return mat_a, mat_b, response, mirror * (1.0 / math.sqrt(block_len))
 
     def spread(o, i, value):
         q = i % 2
-        return value, to_chips(o, value, q), to_cores(o, value, q, True)
+        return value, to_chips(o, value, q), to_cores(value)
 
     def branch(o):
         spans = spans_of(PIECES_ONCE if o == top else PIECES)
@@ -624,7 +627,7 @@
             list(spread(o, i, seeded(o, x, pieces[i], col_facts))) for i, x in enumerate(came)
         ]
         for i, now in enumerate(spreads[:-1]):
-            now.append(to_cores(o, now[1], i % 2, False))
+            now.append(to_cores(now[1]))
         return computed(o, spans, pieces, spreads, col_facts, row_facts, o == top)
 
     if half <= BRANCHES:
@@ -637,7 +640,7 @@
         for i, x in enumerate(out_of_block(o, pieces, False)):
             value = seeded(o, x, pieces[i], None)
             value, r2, r3 = spread(o, i, value)
-            r4 = to_cores(o, r2, i % 2, False)
+            r4 = to_cores(r2)
             spreads.append(everywhere(o, value, r2, r3, r4, i % 2))
         return spreads
 

time: 68.1 us -> 92.3 us (1.36)
  waiting for transfers between devices: 4.12 us -> 28.3 us
  Pallas kernels: 12.4 us -> 31.1 us
  starting transfers between devices: 43.9 us -> 25.3 us
    ppermute x13 -> x11, starting transfers between devices: 41.7 us -> 19.8 us  [the longest x5 12.4 us: both_sums(): part = part + lax.ppermute(part, axis, [(i, i ^ step) for i in range(size)])]
    ppermute x13 -> x11, waiting for transfers between devices: 4.11 us -> 16.7 us  [the longest x2 10.8 us: out_of_block(): lax.ppermute(x, 'col', [(o, half + i % 2), (top, half + 2 + i % 2)])]
    ppermute x2, waiting for transfers between devices: 0.01 us -> 11.6 us  [to_chips(): return lax.ppermute(value, 'col', pairs)]
    pallas_call x1, Pallas kernels: 1.35 us -> 9.71 us  [computed(): pl.pallas_call(functools.partial(first_kernel, plan, ahead, len(refs)), o...]
    pallas_call x1, Pallas kernels: 2.65 us -> 10.2 us  [computed(): pl.pallas_call(functools.partial(last_kernel, plan, twice, len(refs)), ou...]
    ppermute x2, starting transfers between devices: 2.18 us -> 5.51 us  [to_chips(): return lax.ppermute(value, 'col', pairs)]
    pallas_call x1, Pallas kernels: 0.11 us -> 2.43 us  [after(): pl.pallas_call(pass_kernel, out_shape=pltpu.VMEM(value.shape, value.dtype...]
  transfers between devices with their start and end apart: 15 -> 13, of which waited for: 3 -> 7; matrix products, arithmetic and copies ran while one was open for 2% -> 1% of each run, Pallas kernels for 11% -> 20%
where the time goes in v1:
time: 92.3 us; the launch traced here: 91.4 us
  Pallas kernels  31.1 us (34%)
  waiting for transfers between devices  28.3 us (31%)
  starting transfers between devices  25.3 us (27%)
  between operations  2.79 us (3%)
  local copies, waits for them, and re-layouts  2.1 us (2%)
  other arithmetic  1.3 us (1%)
    ppermute x5, starting transfers between devices, both_sums(): part = part + lax.ppermute(part, axis, [(i, i ^ step) for i in range(size)])  12.4 us
    ppermute x2, waiting for transfers between devices, to_chips(): return lax.ppermute(value, 'col', pairs)  11.6 us
    ppermute x2, waiting for transfers between devices, out_of_block(): lax.ppermute(x, 'col', [(o, half + i % 2), (top, half + 2 + i % 2)])  10.8 us
    pallas_call x1, Pallas kernels, computed(): pl.pallas_call(functools.partial(last_kernel, plan, twice, len(refs)), ou...  10.2 us
    pallas_call x1, Pallas kernels, computed(): pl.pallas_call(functools.partial(first_kernel, plan, ahead, len(refs)), o...  9.71 us
    ppermute x2, starting transfers between devices, out_of_block(): lax.ppermute(x, 'col', [(o, half + i % 2), (top, half + 2 + i % 2)])  7.37 us
    ppermute x2, starting transfers between devices, to_chips(): return lax.ppermute(value, 'col', pairs)  5.51 us
    pallas_call x1, Pallas kernels, facts(): pl.pallas_call(functools.partial(facts_kernel, spans), out_shape=[pltpu.V...  3.83 us
  transfers between devices with their start and end apart: 13, of which 7 were waited for; matrix products, arithmetic and copies ran while one was open for 1% of the time, Pallas kernels for 20%

profile of v1, /device:TPU:0, one launch (start us, length us, event | category | flops | bytes accessed | tf_op | source)
XLA Modules:
  0.0 91.4 jit_solution(8053313504003806328)
XLA Ops:
  0.7 1.3 %fusion.1 = (s32[1]{0:T(128)}, s32[1]{0:T(128)}) fusion(s32[2]{0:T(128)} %param.23), kind=kLoop, calls=%fused_computation.20 | loop fusion | bytes 16 | tf_op jit(solution)/shard_map/slice | solution.py:372
  4.1 0.1 stack.123
  4.2 70.7 %conditional.1 = (f32[2,240,960]{2,1,0:T(8,128)}, f32[2,240,960]{2,1,0:T(8,128)}, f32[2,240]{1,0:T(2,128)S(1)}, f32[2,960]{1,0:T(2,128)S(1)}) conditional(s32[]{:T(128)} %clamp.3, (s32[7680,2]{0,1:T(2,128)}, s32[7680]{0:T(1024)}, f32[7680]{0:T(1024)}, f32[7680]{0:T(1024)}, f32[1024]{0:T(1024)}, ...), branch_computations={%region_0.1_spmd, %region_1.2_spmd, %region_2.3_spmd, %region_3.4_... | conditional | flops 4246766848 | bytes 43446152 | solution.py:634
  4.3 1.9 %cut.4.instead.rest_4_.rest_5_ = bf16[240,2304]{1,0:T(8,128)(2,1)S(1)} custom-call(s32[15]{0:T(128)S(1)} %get-tuple-element.80.flags, bf16[960,4500]{1,0:T(8,128)(2,1)} %get-tuple-element.87.dens.rest_6_), custom_call_target="tpu_custom_call" | custom-call | tf_op jit(solution)/shard_map/cond/branch_0_fun/cut/pallas_call | solution.py:424
  6.2 4.9 %collective-permute-start.2 = (bf16[240,2304]{1,0:T(8,128)(2,1)S(1)}, bf16[240,2304]{1,0:T(8,128)(2,1)S(1)}, u32[]{:S(2)}, u32[]{:S(2)}) collective-permute-start(bf16[240,2304]{1,0:T(8,128)(2,1)S(1)} %cut.4.instead.rest_4_.rest_5_), channel_id=1, source_target_pairs={{0,4},{3,6},{8,12},{11,14},{16,20},{19,22},{24,28},{27,30}} | collective-permute-start | bytes 3317768 | tf_op jit(solution)/shard_map/cond/branch_0_fun/ppermute | solution.py:494
  11.4 0.3 stack.45
  11.8 3.8 %facts.4 = (f32[8,960]{1,0:T(8,128)S(1)}, f32[2,240,128]{2,1,0:T(8,128)S(1)}, bf16[240,2304]{1,0:T(8,128)(2,1)S(1)}) custom-call(s32[15]{0:T(128)S(1)} %get-tuple-element.80.flags, f32[8,7936]{1,0:T(8,128)S(1)} %pad.12.packed, f32[16,128]{1,0:T(8,128)S(1)} %pad_maximum_fusion.1.table, bf16[960,4500]{1,0:T(8,128)(2,1)} %get-tuple-element.87.dens.rest_6_), custom_call_target="tpu_custom_call" | custom-call | flops 1 | bytes 1 | tf_op jit(solution)/shard_map/cond/branch_0_fun/facts/pallas_call | solution.py:526
  15.6 8.4 %collective-permute-done.2.value = bf16[240,2304]{1,0:T(8,128)(2,1)S(1)} collective-permute-done((bf16[240,2304]{1,0:T(8,128)(2,1)S(1)}, bf16[240,2304]{1,0:T(8,128)(2,1)S(1)}, u32[]{:S(2)}, u32[]{:S(2)}) %collective-permute-start.2) | collective-permute-done | bytes 1105952 | tf_op jit(solution)/shard_map/cond/branch_0_fun/ppermute | solution.py:494
  24.0 0.7 seed.9.rest_0_
  24.7 2.3 %collective-permute-start.3 = (bf16[240,2304]{1,0:T(8,128)(2,1)S(1)}, bf16[240,2304]{1,0:T(8,128)(2,1)}, u32[]{:S(2)}, u32[]{:S(2)}) collective-permute-start(bf16[240,2304]{1,0:T(8,128)(2,1)S(1)} %seed.9.rest_0_), channel_id=1, source_target_pairs={{4,6},{6,4},{0,2},{12,14},{14,12},{8,10},{20,22},{22,20},{16,18},{... | collective-permute-start | bytes 3317768 | tf_op jit(solution)/shard_map/cond/branch_0_fun/ppermute | solution.py:465
  27.0 2.4 %collective-permute-start = (bf16[240,2304]{1,0:T(8,128)(2,1)S(1)}, bf16[240,2304]{1,0:T(8,128)(2,1)}, u32[]{:S(2)}, u32[]{:S(2)}) collective-permute-start(bf16[240,2304]{1,0:T(8,128)(2,1)S(1)} %get-tuple-element.88.instead.rest_4_.rest_5_), channel_id=1, source_target_pairs={{0,5},{3,7},{8,13},{11,15},{16,21},{19,23},{24,29},{27,31}} | collective-permute-start | bytes 3317768 | tf_op jit(solution)/shard_map/cond/branch_0_fun/ppermute | solution.py:494
  29.4 9.5 %collective-permute-done.3.rest_1_ = bf16[240,2304]{1,0:T(8,128)(2,1)} collective-permute-done((bf16[240,2304]{1,0:T(8,128)(2,1)S(1)}, bf16[240,2304]{1,0:T(8,128)(2,1)}, u32[]{:S(2)}, u32[]{:S(2)}) %collective-permute-start.3) | collective-permute-done | bytes 1105952 | tf_op jit(solution)/shard_map/cond/branch_0_fun/ppermute | solution.py:465
  38.9 2.4 %collective-permute-done.value = bf16[240,2304]{1,0:T(8,128)(2,1)} collective-permute-done((bf16[240,2304]{1,0:T(8,128)(2,1)S(1)}, bf16[240,2304]{1,0:T(8,128)(2,1)}, u32[]{:S(2)}, u32[]{:S(2)}) %collective-permute-start) | collective-permute-done | bytes 1105952 | tf_op jit(solution)/shard_map/cond/branch_0_fun/ppermute | solution.py:494
  41.3 2.4 %seed.8.rest_0_ = bf16[240,2304]{1,0:T(8,128)(2,1)} custom-call(s32[15]{0:T(128)S(1)} %get-tuple-element.80.flags, bf16[240,2304]{1,0:T(8,128)(2,1)} %collective-permute-done.value, bf16[240,2304]{1,0:T(8,128)(2,1)S(1)} %get-tuple-element.88.instead.rest_4_.rest_5_, f32[8,960]{1,0:T(8,128)S(1)} %get-tuple-element.89.token.rest_8_), custom_call_target="tpu_custom_call", output_to_operand_aliasing={{}: (1, {})} | custom-call | flops 1 | bytes 1 | tf_op jit(solution)/shard_map/cond/branch_0_fun/seed/pallas_call | solution.py:450
  43.7 3.2 %collective-permute-start.1 = (bf16[240,2304]{1,0:T(8,128)(2,1)}, bf16[240,2304]{1,0:T(8,128)(2,1)}, u32[]{:S(2)}, u32[]{:S(2)}) collective-permute-start(bf16[240,2304]{1,0:T(8,128)(2,1)} %seed.8.rest_0_), channel_id=1, source_target_pairs={{5,7},{7,5},{0,3},{13,15},{15,13},{8,11},{21,23},{23,21},{16,19},{... | collective-permute-start | bytes 3317768 | tf_op jit(solution)/shard_map/cond/branch_0_fun/ppermute | solution.py:465
  46.9 0.1 reshape.143
  47.0 0.1 reshape.144
  47.2 0.1 collective-permute-start.6
  47.3 9.7 %first.4 = (f32[960,960]{1,0:T(8,128)S(1)}, f32[8,128]{1,0:T(8,128)S(1)}, bf16[960,4500]{1,0:T(8,128)(2,1)S(1)}) custom-call(s32[15]{0:T(128)S(1)} %get-tuple-element.80.flags, bf16[240,2304]{1,0:T(8,128)(2,1)S(1)} %seed.9.rest_0_, bf16[240,2304]{1,0:T(8,128)(2,1)} %collective-permute-done.3.rest_1_, bf16[240,2304]{1,0:T(8,128)(2,1)} %collective-permute-done.4.rest_2_, ...), custom_call_target="tpu_custom_call" | custom-call | flops 1 | bytes 1 | tf_op jit(solution)/shard_map/cond/branch_0_fun/first/pallas_call | solution.py:566
  57.0 2.1 %collective-permute-done.1.value = bf16[240,2304]{1,0:T(8,128)(2,1)} collective-permute-done((bf16[240,2304]{1,0:T(8,128)(2,1)}, bf16[240,2304]{1,0:T(8,128)(2,1)}, u32[]{:S(2)}, u32[]{:S(2)}) %collective-permute-start.1) | collective-permute-done | bytes 1105952 | tf_op jit(solution)/shard_map/cond/branch_0_fun/ppermute | solution.py:465
  59.1 2.4 %after.4.rest_1_ = bf16[240,2304]{1,0:T(8,128)(2,1)} custom-call(bf16[240,2304]{1,0:T(8,128)(2,1)} %collective-permute-done.1.value, f32[8,128]{1,0:T(8,128)S(1)} %get-tuple-element.92.token), custom_call_target="tpu_custom_call", output_to_operand_aliasing={{}: (0, {})} | custom-call | flops 1 | bytes 1 | tf_op jit(solution)/shard_map/cond/branch_0_fun/after/pallas_call | solution.py:506
  61.5 2.9 %collective-permute-done.7.rest_3_ = bf16[240,2304]{1,0:T(8,128)(2,1)S(1)} collective-permute-done((bf16[240,2304]{1,0:T(8,128)(2,1)}, bf16[240,2304]{1,0:T(8,128)(2,1)S(1)}, u32[]{:S(2)}, u32[]{:S(2)}) %collective-permute-start.7) | collective-permute-done | bytes 1105952 | tf_op jit(solution)/shard_map/cond/branch_0_fun/ppermute | solution.py:468
  64.5 10.2 %last.4 = (f32[2,240,960]{2,1,0:T(8,128)}, f32[2,240,960]{2,1,0:T(8,128)}, f32[2,240]{1,0:T(2,128)S(1)}, f32[2,960]{1,0:T(2,128)S(1)}, f32[960,960]{1,0:T(8,128)S(1)}) custom-call(s32[15]{0:T(128)S(1)} %get-tuple-element.80.flags, bf16[240,2304]{1,0:T(8,128)(2,1)} %seed.8.rest_0_, bf16[240,2304]{1,0:T(8,128)(2,1)} %after.4.rest_1_, ...), custom_call_target="tpu_custom_call", output_to_operand_aliasing={{4}: (11, {})} | custom-call | flops 4246732800 | bytes 3686400 | tf_op jit(solution)/shard_map/cond/branch_0_fun/last/pallas_call | solution.py:586
  74.9 0.2 collective-permute-start.34
  75.1 1.6 %collective-permute-start.37 = (f32[2,960]{1,0:T(2,128)S(1)}, f32[2,960]{1,0:T(2,128)S(1)}, u32[]{:S(2)}, u32[]{:S(2)}) collective-permute-start(f32[2,960]{1,0:T(2,128)S(1)} %get-tuple-element.174), channel_id=1, source_target_pairs={{0,8},{8,0},{16,24},{24,16},{1,9},{9,1},{17,25},{25,17},{2,10},{10... | collective-permute-start | bytes 23048 | tf_op jit(solution)/shard_map/ppermute | solution.py:342
  76.7 3.3 %collective-permute-start.35 = (f32[2,256]{1,0:T(2,128)S(1)}, f32[2,256]{1,0:T(2,128)S(1)}, u32[]{:S(2)}, u32[]{:S(2)}) collective-permute-start(f32[2,256]{1,0:T(2,128)S(1)} %pad_add_fusion), channel_id=1, source_target_pairs={{0,2},{1,3},{2,0},{3,1},{4,6},{5,7},{6,4},{7,5},{8,10},{9,11},{10,... | collective-permute-start | bytes 6152 | tf_op jit(solution)/shard_map/ppermute | solution.py:342
  80.0 1.6 %collective-permute-done.35 = f32[2,256]{1,0:T(2,128)S(1)} collective-permute-done((f32[2,256]{1,0:T(2,128)S(1)}, f32[2,256]{1,0:T(2,128)S(1)}, u32[]{:S(2)}, u32[]{:S(2)}) %collective-permute-start.35) | collective-permute-done | bytes 2080 | tf_op jit(solution)/shard_map/ppermute | solution.py:342
  81.6 4.6 %collective-permute-start.36 = (f32[2,256]{1,0:T(2,128)S(1)}, f32[2,256]{1,0:T(2,128)S(1)}, u32[]{:S(2)}, u32[]{:S(2)}) collective-permute-start(f32[2,256]{1,0:T(2,128)S(1)} %add.49), channel_id=1, source_target_pairs={{0,4},{1,5},{2,6},{3,7},{4,0},{5,1},{6,2},{7,3},{8,12},{9,13},{10,... | collective-permute-start | bytes 6152 | tf_op jit(solution)/shard_map/ppermute | solution.py:342
  86.2 2.7 %collective-permute-start.38 = (f32[2,960]{1,0:T(2,128)S(1)}, f32[2,960]{1,0:T(2,128)S(1)}, u32[]{:S(2)}, u32[]{:S(2)}) collective-permute-start(f32[2,960]{1,0:T(2,128)S(1)} %add.51), channel_id=1, source_target_pairs={{0,16},{8,24},{16,0},{24,8},{1,17},{9,25},{17,1},{25,9},{2,18},{10... | collective-permute-start | bytes 23048 | tf_op jit(solution)/shard_map/ppermute | solution.py:342
  88.9 0.6 fusion
  89.4 1.4 %collective-permute-done.38 = f32[2,960]{1,0:T(2,128)S(1)} collective-permute-done((f32[2,960]{1,0:T(2,128)S(1)}, f32[2,960]{1,0:T(2,128)S(1)}, u32[]{:S(2)}, u32[]{:S(2)}) %collective-permute-start.38) | collective-permute-done | bytes 7712 | tf_op jit(solution)/shard_map/ppermute | solution.py:342
  90.8 0.6 add_multiply_fusion
  (43 shorter events, 0.3 us)
Async XLA Ops:
  4.2 6.9 %copy-start.16 = (f32[7680]{0:T(1024)S(1)}, f32[7680]{0:T(1024)}, u32[]{:S(2)}) copy-start(f32[7680]{0:T(1024)} %get-tuple-element.83) | copy-start | bytes 92164 | tf_op jit(solution)/shard_map/cond
  4.2 7.0 %copy-start.20 = (f32[7680]{0:T(1024)S(1)}, f32[7680]{0:T(1024)}, u32[]{:S(2)}) copy-start(f32[7680]{0:T(1024)} %get-tuple-element.84) | copy-start | bytes 92164 | tf_op jit(solution)/shard_map/cond
  4.2 7.0 %copy-start.12 = (s32[7680]{0:T(1024)S(1)}, s32[7680]{0:T(1024)}, u32[]{:S(2)}) copy-start(s32[7680]{0:T(1024)} %get-tuple-element.82) | copy-start | bytes 92164 | tf_op jit(solution)/shard_map/cond
  4.2 7.0 %copy-start.8 = (s32[7680,2]{0,1:T(2,128)S(1)}, s32[7680,2]{0,1:T(2,128)}, u32[]{:S(2)}) copy-start(s32[7680,2]{0,1:T(2,128)} %get-tuple-element.81) | copy-start | bytes 184324 | tf_op jit(solution)/shard_map/cond
  4.2 7.5 %copy-start.32 = (f32[1024]{0:T(1024)S(1)}, f32[1024]{0:T(1024)}, u32[]{:S(2)}) copy-start(f32[1024]{0:T(1024)} %get-tuple-element.85) | copy-start | bytes 12292 | tf_op jit(solution)/shard_map/cond
  4.2 7.5 %copy-start.36 = (f32[1024]{0:T(1024)S(1)}, f32[1024]{0:T(1024)}, u32[]{:S(2)}) copy-start(f32[1024]{0:T(1024)} %get-tuple-element.86) | copy-start | bytes 12292 | tf_op jit(solution)/shard_map/cond
  6.2 17.8 %collective-permute-start.2 = (bf16[240,2304]{1,0:T(8,128)(2,1)S(1)}, bf16[240,2304]{1,0:T(8,128)(2,1)S(1)}, u32[]{:S(2)}, u32[]{:S(2)}) collective-permute-start(bf16[240,2304]{1,0:T(8,128)(2,1)S(1)} %cut.4.instead.rest_4_.rest_5_), channel_id=1, source_target_pairs={{0,4},{3,6},{8,12},{11,14},{16,20},{19,22},{24,28},{27,30}} | collective-permute-start | bytes 3317768 | tf_op jit(solution)/shard_map/cond/branch_0_fun/ppermute | solution.py:494
  15.6 9.0 %copy-start = (f32[2,240,128]{2,1,0:T(8,128)}, f32[2,240,128]{2,1,0:T(8,128)S(1)}, u32[]{:S(2)}) copy-start(f32[2,240,128]{2,1,0:T(8,128)S(1)} %get-tuple-element.94.rest_9_) | copy-start | bytes 737284 | tf_op jit(solution)/shard_map/cond
  24.7 14.2 %collective-permute-start.3 = (bf16[240,2304]{1,0:T(8,128)(2,1)S(1)}, bf16[240,2304]{1,0:T(8,128)(2,1)}, u32[]{:S(2)}, u32[]{:S(2)}) collective-permute-start(bf16[240,2304]{1,0:T(8,128)(2,1)S(1)} %seed.9.rest_0_), channel_id=1, source_target_pairs={{4,6},{6,4},{0,2},{12,14},{14,12},{8,10},{20,22},{22,20},{16,18},{... | collective-permute-start | bytes 3317768 | tf_op jit(solution)/shard_map/cond/branch_0_fun/ppermute | solution.py:465
  27.0 19.9 %copy-start.24 = (f32[5,900]{1,0:T(8,128)S(1)}, f32[5,900]{1,0:T(8,128)}, u32[]{:S(2)}) copy-start(f32[5,900]{1,0:T(8,128)} %get-tuple-element.90) | copy-start | bytes 54004 | tf_op jit(solution)/shard_map/cond
  27.0 20.0 %copy-start.28 = (f32[5,900]{1,0:T(8,128)S(1)}, f32[5,900]{1,0:T(8,128)}, u32[]{:S(2)}) copy-start(f32[5,900]{1,0:T(8,128)} %get-tuple-element.91) | copy-start | bytes 54004 | tf_op jit(solution)/shard_map/cond
  27.0 14.3 %collective-permute-start = (bf16[240,2304]{1,0:T(8,128)(2,1)S(1)}, bf16[240,2304]{1,0:T(8,128)(2,1)}, u32[]{:S(2)}, u32[]{:S(2)}) collective-permute-start(bf16[240,2304]{1,0:T(8,128)(2,1)S(1)} %get-tuple-element.88.instead.rest_4_.rest_5_), channel_id=1, source_target_pairs={{0,5},{3,7},{8,13},{11,15},{16,21},{19,23},{24,29},{27,31}} | collective-permute-start | bytes 3317768 | tf_op jit(solution)/shard_map/cond/branch_0_fun/ppermute | solution.py:494
  29.4 17.8 %collective-permute-start.4 = (bf16[240,2304]{1,0:T(8,128)(2,1)S(1)}, bf16[240,2304]{1,0:T(8,128)(2,1)}, u32[]{:S(2)}, u32[]{:S(2)}) collective-permute-start(bf16[240,2304]{1,0:T(8,128)(2,1)S(1)} %seed.9.rest_0_), channel_id=1, source_target_pairs={{0,1},{1,0},{2,3},{3,2},{4,5},{5,4},{6,7},{7,6},{8,9},{9,8},{10,11... | collective-permute-start | bytes 3317768 | tf_op jit(solution)/shard_map/cond/branch_0_fun/ppermute | solution.py:468
  38.9 8.4 %collective-permute-start.5 = (bf16[240,2304]{1,0:T(8,128)(2,1)}, bf16[240,2304]{1,0:T(8,128)(2,1)}, u32[]{:S(2)}, u32[]{:S(2)}) collective-permute-start(bf16[240,2304]{1,0:T(8,128)(2,1)} %collective-permute-done.3.rest_1_), channel_id=1, source_target_pairs={{0,1},{1,0},{2,3},{3,2},{4,5},{5,4},{6,7},{7,6},{8,9},{9,8},{10,11... | collective-permute-start | bytes 3317768 | tf_op jit(solution)/shard_map/cond/branch_0_fun/ppermute | solution.py:468
  43.7 15.4 %collective-permute-start.1 = (bf16[240,2304]{1,0:T(8,128)(2,1)}, bf16[240,2304]{1,0:T(8,128)(2,1)}, u32[]{:S(2)}, u32[]{:S(2)}) collective-permute-start(bf16[240,2304]{1,0:T(8,128)(2,1)} %seed.8.rest_0_), channel_id=1, source_target_pairs={{5,7},{7,5},{0,3},{13,15},{15,13},{8,11},{21,23},{23,21},{16,19},{... | collective-permute-start | bytes 3317768 | tf_op jit(solution)/shard_map/cond/branch_0_fun/ppermute | solution.py:465
  47.2 14.4 %collective-permute-start.6 = (bf16[240,2304]{1,0:T(8,128)(2,1)}, bf16[240,2304]{1,0:T(8,128)(2,1)S(1)}, u32[]{:S(2)}, u32[]{:S(2)}) collective-permute-start(bf16[240,2304]{1,0:T(8,128)(2,1)} %seed.8.rest_0_), channel_id=1, source_target_pairs={{0,1},{1,0},{2,3},{3,2},{4,5},{5,4},{6,7},{7,6},{8,9},{9,8},{10,11... | collective-permute-start | bytes 3317768 | tf_op jit(solution)/shard_map/cond/branch_0_fun/ppermute | solution.py:468
  59.1 5.4 %copy-start.1 = (f32[2,240,128]{2,1,0:T(8,128)S(1)}, f32[2,240,128]{2,1,0:T(8,128)}, u32[]{:S(2)}) copy-start(f32[2,240,128]{2,1,0:T(8,128)} %copy-done) | copy-start | bytes 737284 | tf_op jit(solution)/shard_map/cond
  61.5 3.0 %collective-permute-start.7 = (bf16[240,2304]{1,0:T(8,128)(2,1)}, bf16[240,2304]{1,0:T(8,128)(2,1)S(1)}, u32[]{:S(2)}, u32[]{:S(2)}) collective-permute-start(bf16[240,2304]{1,0:T(8,128)(2,1)} %after.4.rest_1_), channel_id=1, source_target_pairs={{0,1},{1,0},{2,3},{3,2},{4,5},{5,4},{6,7},{7,6},{8,9},{9,8},{10,11... | collective-permute-start | bytes 3317768 | tf_op jit(solution)/shard_map/cond/branch_0_fun/ppermute | solution.py:468
  74.9 1.8 %collective-permute-start.34 = (f32[2,256]{1,0:T(2,128)S(1)}, f32[2,256]{1,0:T(2,128)S(1)}, u32[]{:S(2)}, u32[]{:S(2)}) collective-permute-start(f32[2,256]{1,0:T(2,128)S(1)} %pad.17), channel_id=1, source_target_pairs={{0,1},{1,0},{2,3},{3,2},{4,5},{5,4},{6,7},{7,6},{8,9},{9,8},{10,11... | collective-permute-start | bytes 6152 | tf_op jit(solution)/shard_map/ppermute | solution.py:342
  75.1 11.1 %collective-permute-start.37 = (f32[2,960]{1,0:T(2,128)S(1)}, f32[2,960]{1,0:T(2,128)S(1)}, u32[]{:S(2)}, u32[]{:S(2)}) collective-permute-start(f32[2,960]{1,0:T(2,128)S(1)} %get-tuple-element.174), channel_id=1, source_target_pairs={{0,8},{8,0},{16,24},{24,16},{1,9},{9,1},{17,25},{25,17},{2,10},{10... | collective-permute-start | bytes 23048 | tf_op jit(solution)/shard_map/ppermute | solution.py:342
  76.7 4.9 %collective-permute-start.35 = (f32[2,256]{1,0:T(2,128)S(1)}, f32[2,256]{1,0:T(2,128)S(1)}, u32[]{:S(2)}, u32[]{:S(2)}) collective-permute-start(f32[2,256]{1,0:T(2,128)S(1)} %pad_add_fusion), channel_id=1, source_target_pairs={{0,2},{1,3},{2,0},{3,1},{4,6},{5,7},{6,4},{7,5},{8,10},{9,11},{10,... | collective-permute-start | bytes 6152 | tf_op jit(solution)/shard_map/ppermute | solution.py:342
  81.6 7.3 %collective-permute-start.36 = (f32[2,256]{1,0:T(2,128)S(1)}, f32[2,256]{1,0:T(2,128)S(1)}, u32[]{:S(2)}, u32[]{:S(2)}) collective-permute-start(f32[2,256]{1,0:T(2,128)S(1)} %add.49), channel_id=1, source_target_pairs={{0,4},{1,5},{2,6},{3,7},{4,0},{5,1},{6,2},{7,3},{8,12},{9,13},{10,... | collective-permute-start | bytes 6152 | tf_op jit(solution)/shard_map/ppermute | solution.py:342
  86.2 4.6 %collective-permute-start.38 = (f32[2,960]{1,0:T(2,128)S(1)}, f32[2,960]{1,0:T(2,128)S(1)}, u32[]{:S(2)}, u32[]{:S(2)}) collective-permute-start(f32[2,960]{1,0:T(2,128)S(1)} %add.51), channel_id=1, source_target_pairs={{0,16},{8,24},{16,0},{24,8},{1,17},{9,25},{17,1},{25,9},{2,18},{10... | collective-permute-start | bytes 23048 | tf_op jit(solution)/shard_map/ppermute | solution.py:342
